TPU v7x, 256 devices: a whole 4x4x8 slice. The times are simulated.
256 devices in a mesh: seq: 32 (over z, x), head: 8 (over y, core).
Axes of the slice: x: 4, y: 4, z: 8, core: 2. Of those that a mesh axis runs over, the one named last changes fastest.
Arguments:
- mixer_input: bfloat16 [65536, 5120], P('seq', 'head'), may hold values from -6 to 6
- write_rows: bfloat16 [65536, 128], P(('seq', 'head')), may hold values from -1.796875 to 1.796875
- read_rows: bfloat16 [65536, 128], P(('seq', 'head')), may hold values from -1.796875 to 1.796875
- log_decay: float32 [80, 65536], P('head', 'seq'), may hold values from -2 to 0, as said below
- skip_gain: float32 [80], P('head'), may hold values from 0.25 to 1.75
- reset_offsets: int32 [32, 4], P('seq'), may hold values from 0 to 2048, as said below
- grad_out: bfloat16 [65536, 5120], P('seq', 'head'), may hold values from -6 to 6
Outputs:
- grad_input: bfloat16 [65536, 5120], P('seq', 'head')
- grad_write: float32 [65536, 128], P(('seq', 'head'))
- grad_read: float32 [65536, 128], P(('seq', 'head'))
Inputs may be any that keep to these rules, and one draw needn't show every extreme that they name: `log_decay`: every entry is negative. `reset_offsets`: row d lists, in increasing order, the offsets within block d of 2048 tokens at which an episode begins; unused slots hold 2048 and stand after the used ones; some row uses all 4 slots.
All inputs are finite; a program needn't handle non-finite values.
Results may differ from a plain program's by a relative error of at most 0.0055.
Values may be sent and summed in bfloat16 or wider, within the bound.
No kernel may reach another device: no remote copies, remote signals or barrier semaphores. Data moves between devices by JAX's collectives and lax.ppermute only.
A program may use at most 192 MiB of HBM per device.

v0:
```python
import jax
import jax.numpy as jnp
from jax import lax
from jax.sharding import PartitionSpec as P

SPAN = 256


def entering(part, axis, combine, identity, reverse):
    count = lax.axis_size(axis)
    place = lax.axis_index(axis)
    ahead = count - 1 - place if reverse else place
    gathered = jax.tree.map(lambda a: lax.all_gather(a, axis), part)
    state = jax.tree.map(lambda a, e: jnp.zeros_like(a) + jnp.asarray(e, a.dtype), part, identity)

    def one(step, state):
        source = count - 1 - step if reverse else step
        return combine(
            state, jax.tree.map(lambda a: lax.dynamic_index_in_dim(a, source, 0, False), gathered)
        )

    return lax.fori_loop(0, ahead, one, state)


def span_update(carry_state, inputs, skip_gain):
    feature_part, write_part, read_part, log_part, reset_part = inputs
    span_len = reset_part.shape[0]
    cum_log = jnp.cumsum(log_part, axis=1)
    reset_count = jnp.cumsum(reset_part)
    input_gain = jnp.sqrt(-jnp.expm1(2.0 * log_part))
    positions = jnp.arange(span_len)
    allowed = (positions[:, None] >= positions[None, :]) & (
        reset_count[:, None] == reset_count[None, :]
    )
    spread = cum_log[:, :, None] - cum_log[:, None, :]
    decay_matrix = jnp.exp(jnp.where(allowed[None], spread, -1e30))
    scores = jnp.dot(read_part, write_part.T, precision=lax.Precision.HIGHEST)
    weights = decay_matrix * scores[None] * input_gain[:, None, :]
    result = jnp.einsum("hts,shp->thp", weights, feature_part, precision=lax.Precision.HIGHEST)
    entry_decay = jnp.exp(cum_log) * (reset_count == 0)[None, :]
    carried = jnp.einsum("tn,hnp->thp", read_part, carry_state, precision=lax.Precision.HIGHEST)
    result = result + carried * entry_decay.T[:, :, None] + skip_gain[None, :, None] * feature_part
    tail_weight = (
        jnp.exp(cum_log[:, -1:] - cum_log) * (reset_count == reset_count[-1])[None, :] * input_gain
    )
    block_decay = jnp.exp(cum_log[:, -1]) * (reset_count[-1] == 0)
    fresh_state = jnp.einsum(
        "sn,shp->hnp",
        write_part,
        feature_part * tail_weight.T[:, :, None],
        precision=lax.Precision.HIGHEST,
    )
    return (block_decay[:, None, None] * carry_state + fresh_state, result)


def link_states(earlier, later):
    return (earlier[0] * later[0], later[0][:, None, None] * earlier[1] + later[1])


def shards(mixer_input, write_rows, read_rows, log_decay, skip_gain, reset_offsets, grad_out):
    write_whole, read_whole = (
        lax.all_gather(write_rows, "head", axis=0, tiled=True),
        lax.all_gather(read_rows, "head", axis=0, tiled=True),
    )
    token_count = mixer_input.shape[0]
    head_count = log_decay.shape[0]
    head_width = mixer_input.shape[1] // head_count
    feature_full = mixer_input.astype(jnp.float32).reshape(token_count, head_count, head_width)
    write_full = write_whole.astype(jnp.float32)
    read_full = read_whole.astype(jnp.float32)
    cotangent = grad_out.astype(jnp.float32).reshape(token_count, head_count, head_width)
    positions = jnp.arange(token_count, dtype=jnp.int32)
    resets = jnp.any(positions[:, None] == reset_offsets[0][None, :], axis=1).astype(jnp.float32)
    cum_log = jnp.cumsum(log_decay, axis=1)
    reset_count = jnp.cumsum(resets)
    input_gain = jnp.sqrt(-jnp.expm1(2.0 * log_decay))
    tail_weight = (
        jnp.exp(cum_log[:, -1:] - cum_log) * (reset_count == reset_count[-1])[None, :] * input_gain
    )
    local_state = jnp.einsum(
        "tn,thp->hnp",
        write_full,
        feature_full * tail_weight.T[:, :, None],
        precision=lax.Precision.HIGHEST,
    )
    block_decay = jnp.exp(cum_log[:, -1]) * (reset_count[-1] == 0)
    entry_decay = jnp.exp(cum_log) * (reset_count == 0)[None, :]
    local_grad = jnp.einsum(
        "tn,thp->hnp",
        read_full,
        cotangent * entry_decay.T[:, :, None],
        precision=lax.Precision.HIGHEST,
    )
    identity = (jnp.ones_like(block_decay), jnp.zeros_like(local_state))
    decay_before, state_in = entering(
        (block_decay, local_state), "seq", link_states, identity, False
    )
    decay_after, grad_in = entering((block_decay, local_grad), "seq", link_states, identity, True)
    spans = token_count // SPAN
    log_blocks = log_decay.reshape(head_count, spans, SPAN).transpose(1, 0, 2)
    reset_blocks = resets.reshape(spans, SPAN)

    def block_forward(feature_arg, write_arg, read_arg):
        feature_blocks = feature_arg.reshape(spans, SPAN, head_count, head_width)
        write_blocks = write_arg.reshape(spans, SPAN, write_arg.shape[1])
        read_blocks = read_arg.reshape(spans, SPAN, read_arg.shape[1])

        def advance(carry_state, inputs):
            return span_update(carry_state, inputs, skip_gain)

        end_state, outputs = lax.scan(
            advance, state_in, (feature_blocks, write_blocks, read_blocks, log_blocks, reset_blocks)
        )
        return (outputs.reshape(token_count, head_count, head_width), end_state)

    outputs, pullback = jax.vjp(block_forward, feature_full, write_full, read_full)
    grad_feature, grad_write_all, grad_read_all = pullback((cotangent, grad_in))
    grad_write, grad_read = (
        lax.psum_scatter(grad_write_all, "head", scatter_dimension=0, tiled=True),
        lax.psum_scatter(grad_read_all, "head", scatter_dimension=0, tiled=True),
    )
    grad_input = grad_feature.reshape(token_count, head_count * head_width).astype(jnp.bfloat16)
    return (grad_input, grad_write, grad_read)


def solution(mesh):
    in_specs = (
        P("seq", "head"),
        P(("seq", "head"), None),
        P(("seq", "head"), None),
        P("head", "seq"),
        P("head"),
        P("seq", None),
        P("seq", "head"),
    )
    out_specs = (P("seq", "head"), P(("seq", "head"), None), P(("seq", "head"), None))
    return jax.shard_map(shards, mesh=mesh, in_specs=in_specs, out_specs=out_specs, check_vma=False)
```

profile of v0, /device:TPU:4, one launch (start us, length us, event | category | flops | bytes accessed | tf_op | source)
XLA Modules:
  0.0 574.7 jit_solution(11024643300926106177)
XLA Ops:
  14.8 3.0 copy.74
  18.5 13.6 %all_gather.28 = bf16[2048,128]{1,0:T(8,128)(2,1)S(1)} all-gather(bf16[256,128]{1,0:T(8,128)(2,1)S(1)} %copy-done.5), channel_id=1, replica_groups=mesh['seq'=32,'head'=8] {'head'}, dimensions={0}, use_global_device_ids=true | all-gather | bytes 589824 | tf_op jit(solution)/shard_map/all_gather | solution.py:62
  33.1 3.3 fusion.90
  36.5 3.0 copy.72
  40.3 13.2 %all_gather.25 = bf16[2048,128]{1,0:T(8,128)(2,1)S(1)} all-gather(bf16[256,128]{1,0:T(8,128)(2,1)S(1)} %copy-done.6), channel_id=1, replica_groups=mesh['seq'=32,'head'=8] {'head'}, dimensions={0}, use_global_device_ids=true | all-gather | bytes 589824 | tf_op jit(solution)/shard_map/all_gather | solution.py:63
  53.5 3.3 fusion.87
  60.3 74.4 %all-reduce = f32[320]{0:T(512)S(1)} all-reduce(f32[320]{0:T(512)S(1)} %dynamic-update-slice), channel_id=2, replica_groups=mesh['seq'=32,'head'=8] {'seq'}, use_global_device_ids=true, to_apply=%add | all-reduce | flops 320 | bytes 2560
  134.8 5.0 copy.94
  139.8 3.9 copy.78
  144.9 7.4 %copy.95 = f32[80,8,8,256]{3,2,1,0:T(8,128)} copy(f32[80,8,8,256]{3,1,2,0:T(8,128)} %bitcast.375) | data formatting | bytes 10485760
  155.5 115.7 %while.83 = (s32[]{:T(128)}, f32[10,128,64]{1,2,0:T(8,128)S(1)}, f32[8,128,256]{1,2,0:T(8,128)}, f32[8,10,256,256]{3,2,1,0:T(8,128)}, f32[8,10,1,256]{3,1,2,0:T(...) while((s32[]{:T(128)}, f32[10,128,64]{1,2,0:T(8,128)S(1)}, ...), condition=%wide.region_14.15_spmd.clone.clone, body=%wide.region_9.14_spmd.clone.sunk.clone | while | flops 356031040 | bytes 10219655 | solution.py:111
  158.5 3.1 multiply_dynamic-update-slice_fusion.3
  172.9 3.1 multiply_dynamic-update-slice_fusion.3
  187.5 3.0 multiply_dynamic-update-slice_fusion.3
  201.9 3.0 multiply_dynamic-update-slice_fusion.3
  216.4 3.0 multiply_dynamic-update-slice_fusion.3
  230.9 3.0 multiply_dynamic-update-slice_fusion.3
  245.3 3.0 multiply_dynamic-update-slice_fusion.3
  259.8 2.9 multiply_dynamic-update-slice_fusion.3
  271.2 42.5 %while.80 = (s32[]{:T(128)}, f32[10,128,64]{2,1,0:T(8,128)S(1)}, s32[]{:T(128)}, f32[32,10]{1,0:T(8,128)S(1)}, f32[32,10,128,64]{2,3,1,0:T(8,128)}) while((s32[]{:T(128)}, f32[10,128,64]{2,1,0:T(8,128)S(1)}, s32[]{:T(128)}, f32[32,10]{1,0:T(8,128)S(1)}, f32[32,10,128,64]{2,3,1,0:T(8,128)}) %tuple.184), condition=%wide.region_6.7_spmd.clone, body=%wide.region_5.6_spmd.sunk.clone | while | flops 163846 | bytes 2293995 | solution.py:22
  315.1 182.8 %while.82 = (s32[]{:T(128)}, f32[10,128,64]{1,2,0:T(8,128)S(1)}, bf16[8,256,10,64]{1,3,2,0:T(8,128)(2,1)}, f32[8,256,128]{2,1,0:T(8,128)S(1)}, f32[8,256,128]{2,...) while((s32[]{:T(128)}, f32[10,128,64]{1,2,0:T(8,128)S(1)}, ...), condition=%wide.region_17.18_spmd.clone, body=%wide.region_15.17_spmd.sunk.clone | while | flops 2217705472 | bytes 16956240 | solution.py:111
  315.1 3.0 constant_dynamic-slice_fusion.18
  319.6 4.2 fusion.184
  323.8 4.4 fusion.185
  337.9 3.0 constant_dynamic-slice_fusion.18
  342.4 4.2 fusion.184
  346.7 4.4 fusion.185
  360.8 3.0 constant_dynamic-slice_fusion.18
  365.3 4.2 fusion.184
  369.5 4.4 fusion.185
  383.6 3.0 constant_dynamic-slice_fusion.18
  388.1 4.2 fusion.184
  392.3 4.4 fusion.185
  406.5 3.0 constant_dynamic-slice_fusion.18
  411.0 4.2 fusion.184
  415.2 4.4 fusion.185
  429.3 3.0 constant_dynamic-slice_fusion.18
  433.8 4.2 fusion.184
  438.0 4.4 fusion.185
  452.2 3.0 constant_dynamic-slice_fusion.18
  456.7 4.2 fusion.184
  460.9 4.4 fusion.185
  475.0 3.0 constant_dynamic-slice_fusion.18
  479.5 4.2 fusion.184
  483.8 4.4 fusion.185
  499.5 3.4 copy.83
  506.3 25.5 %reduce-scatter.3.cloned.1.call-done = f32[256,128]{1,0:T(8,128)} async-done(((f32[2048,128]{1,0:T(8,128)}), f32[256,128]{1,0:T(8,128)}) %reduce-scatter.3.cloned.1.call-update) | async-done | bytes 131088 | tf_op jit(solution)/shard_map/reduce_scatter | solution.py:119
  531.9 36.3 %reduce-scatter.5.cloned.1.call-done = f32[256,128]{1,0:T(8,128)} async-done(((f32[2048,128]{1,0:T(8,128)}), f32[256,128]{1,0:T(8,128)}) %reduce-scatter.5.cloned.1.call-update) | async-done | bytes 131088 | tf_op jit(solution)/shard_map/reduce_scatter | solution.py:120
  (521 shorter events, 241.1 us)
Async XLA Ops:
  7.2 145.1 %all-gather.8.cloned.1.call-start = ((), (), s32[]{:S(2)}) async-start(), calls=%async_computation.5 | async-start | bytes 10813440 | tf_op jit(solution)/shard_map/all_gather | solution.py:13
  14.8 3.7 copy-start.5
  17.8 14.5 %copy-start.3 = (f32[10,2048]{1,0:T(8,128)S(1)}, f32[10,2048]{1,0:T(8,128)}, u32[]{:S(2)}) copy-start(f32[10,2048]{1,0:T(8,128)} %param.18) | copy-start | bytes 245764
  18.5 14.6 %copy-start = (f32[2048,640]{0,1:T(8,128)}, f32[2048,640]{0,1:T(8,128)S(1)}, u32[]{:S(2)}) copy-start(f32[2048,640]{0,1:T(8,128)S(1)} %convert_element_type.76) | copy-start | bytes 15728644
  36.5 3.8 copy-start.6
  36.5 234.6 %all-gather.6.cloned.1.call-start = ((), (), s32[]{:S(2)}) async-start(), calls=%async_computation.4 | async-start | bytes 10813440 | tf_op jit(solution)/shard_map/all_gather | solution.py:13
  39.5 14.0 %copy-start.4 = (f32[2048,10]{0,1:T(8,128)S(1)}, f32[2048,10]{0,1:T(8,128)}, u32[]{:S(2)}) copy-start(f32[2048,10]{0,1:T(8,128)} %get-tuple-element.1043) | copy-start | bytes 245764
  40.2 13.3 %copy-start.1 = (f32[2048,640]{0,1:T(8,128)}, f32[2048,640]{0,1:T(8,128)S(1)}, u32[]{:S(2)}) copy-start(f32[2048,640]{0,1:T(8,128)S(1)} %convert_element_type.74) | copy-start | bytes 15728644
  40.2 18.5 %copy-start.8 = (u32[256]{0:T(256)S(1)}, u32[256]{0:T(256)}, u32[]{:S(2)}) copy-start(u32[256]{0:T(256)} %constant.201) | copy-start | bytes 3076
  56.8 475.0 %reduce-scatter.3.cloned.1.call-start = ((), (), s32[]{:S(2)}) async-start(), calls=%async_computation.2 | async-start | bytes 1179648 | tf_op jit(solution)/shard_map/reduce_scatter | solution.py:119
  271.2 43.9 %copy-start.7 = (f32[10]{0:T(128)S(1)}, f32[10]{0:T(128)}, u32[]{:S(2)}) copy-start(f32[10]{0:T(128)} %param.19) | copy-start | bytes 124
  497.9 1.0 copy-start.2
  498.9 69.3 %reduce-scatter.5.cloned.1.call-start = ((), (), s32[]{:S(2)}) async-start(), calls=%async_computation.3 | async-start | bytes 1179648 | tf_op jit(solution)/shard_map/reduce_scatter | solution.py:120
Sparse Core Ops, SparseCore 0:
  36.6 110.4 all-gather.7
  149.7 105.9 all-gather.5
  499.0 32.8 reduce-scatter.2
  534.8 33.3 reduce-scatter.4
where the time goes:
time: 579 us; the launch traced here: 575 us
  matrix products  184 us (32%)
  local copies, waits for them, and re-layouts  124 us (21%)
  blocking collectives  101 us (17%)
  other arithmetic  78.9 us (14%)
  waiting for transfers between devices  62.2 us (11%)
  between operations  15.4 us (3%)
  loops' own time  8.71 us (2%)
    unnamed x1, blocking collectives  74.4 us
    dot_general x16, matrix products, span_update(): jnp.einsum('hts,shp->thp', weights, feature_part, precision=lax.Precision...  68.6 us
    dynamic_update_slice x32, other arithmetic, block_forward(): lax.scan(advance, state_in, (feature_blocks, write_blocks, read_blocks, l...  45.9 us
    dot_general x24, matrix products, span_update(): jnp.einsum('sn,shp->hnp', write_part, feature_part * tail_weight.T[:, :,...  39.4 us
    dynamic_slice x62, local copies, waits for them, and re-layouts, one(): lax.dynamic_index_in_dim(a, source, 0, False)  38.2 us
    dot_general x24, matrix products, span_update(): scores = jnp.dot(read_part, write_part.T, precision=lax.Precision.HIGHEST)  37.9 us
    reduce_scatter x1, waiting for transfers between devices, shards(): lax.psum_scatter(grad_read_all, 'head', scatter_dimension=0, tiled=True)  36.3 us
    dot_general x16, matrix products, span_update(): jnp.einsum('tn,hnp->thp', read_part, carry_state, precision=lax.Precision...  31.6 us
  transfers between devices with their start and end apart: 4, of which 2 were waited for; matrix products, arithmetic and copies ran while one was open for 25% of the time, Pallas kernels for 0%

commit v1 on v0

--- a/solution.py
+++ b/solution.py
@@ -4,6 +4,27 @@
 from jax.sharding import PartitionSpec as P
 
 SPAN = 256
+
+
+def gather_around(x, axis, dim):
+    devices, mine, span = (lax.axis_size(axis), lax.axis_index(axis), x.shape[dim])
+    upward = [(i, (i + 1) % devices) for i in range(devices)]
+    left = [(i, (i - 1) % devices) for i in range(devices)]
+    out = jnp.zeros((*x.shape[:dim], devices * span, *x.shape[dim + 1 :]), x.dtype)
+    out = lax.dynamic_update_slice_in_dim(out, x, mine * span, axis=dim)
+    from_left = from_right = x
+    middle = devices // 2
+    for step in range(1, middle + 1):
+        from_left = lax.ppermute(from_left, axis, upward)
+        out = lax.dynamic_update_slice_in_dim(
+            out, from_left, (mine - step) % devices * span, axis=dim
+        )
+        if step < devices - middle:
+            from_right = lax.ppermute(from_right, axis, left)
+            out = lax.dynamic_update_slice_in_dim(
+                out, from_right, (mine + step) % devices * span, axis=dim
+            )
+    return out
 
 
 def entering(part, axis, combine, identity, reverse):
@@ -60,7 +81,7 @@
 def shards(mixer_input, write_rows, read_rows, log_decay, skip_gain, reset_offsets, grad_out):
     write_whole, read_whole = (
         lax.all_gather(write_rows, "head", axis=0, tiled=True),
-        lax.all_gather(read_rows, "head", axis=0, tiled=True),
+        gather_around(read_rows, "head", 0),
     )
     token_count = mixer_input.shape[0]
     head_count = log_decay.shape[0]

time: 579 us -> 588 us (1.016)
  blocking collectives: 101 us -> 87.9 us
  starting transfers between devices: 0.43 us -> 9.5 us
  waiting for transfers between devices: 62.2 us -> 68.8 us
  local copies, waits for them, and re-layouts: 124 us -> 130 us
    all_gather x1 -> x0, blocking collectives: 13.2 us -> none  [shards(): lax.all_gather(read_rows, 'head', axis=0, tiled=True)]
    ppermute x0 -> x7, starting transfers between devices: none -> 9.07 us  [the longest x3 8.69 us: gather_around(): from_right = lax.ppermute(from_right, axis, left)]
    ppermute x0 -> x7, waiting for transfers between devices: none -> 8.5 us  [the longest x4 8.35 us: gather_around(): from_left = lax.ppermute(from_left, axis, upward)]
    unnamed x33 -> x35, local copies, waits for them, and re-layouts: 28.9 us -> 30.2 us
  transfers between devices with their start and end apart: 4 -> 11, of which waited for: 2 -> 6; matrix products, arithmetic and copies ran while one was open for 25% -> 26% of each run, Pallas kernels for 0% -> 0%
where the time goes in v1:
time: 588 us; the launch traced here: 582 us
  matrix products  179 us (30%)
  local copies, waits for them, and re-layouts  130 us (22%)
  blocking collectives  87.9 us (15%)
  other arithmetic  84.2 us (14%)
  waiting for transfers between devices  68.8 us (12%)
  between operations  15.5 us (3%)
  starting transfers between devices  9.5 us (2%)
  loops' own time  8.07 us (1%)
    unnamed x1, blocking collectives  74.1 us
    dot_general x16, matrix products, span_update(): jnp.einsum('hts,shp->thp', weights, feature_part, precision=lax.Precision...  68.6 us
    dynamic_update_slice x32, other arithmetic, block_forward(): lax.scan(advance, state_in, (feature_blocks, write_blocks, read_blocks, l...  50.8 us
    dot_general x24, matrix products, span_update(): jnp.einsum('sn,shp->hnp', write_part, feature_part * tail_weight.T[:, :,...  39.5 us
    dynamic_slice x62, local copies, waits for them, and re-layouts, one(): lax.dynamic_index_in_dim(a, source, 0, False)  38.2 us
    reduce_scatter x1, waiting for transfers between devices, shards(): lax.psum_scatter(grad_read_all, 'head', scatter_dimension=0, tiled=True)  36.3 us
    dot_general x24, matrix products, span_update(): scores = jnp.dot(read_part, write_part.T, precision=lax.Precision.HIGHEST)  32.6 us
    dot_general x16, matrix products, span_update(): jnp.einsum('tn,hnp->thp', read_part, carry_state, precision=lax.Precision...  31.6 us
  transfers between devices with their start and end apart: 11, of which 6 were waited for; matrix products, arithmetic and copies ran while one was open for 26% of the time, Pallas kernels for 0%

profile of v1, /device:TPU:4, one launch (start us, length us, event | category | flops | bytes accessed | tf_op | source)
XLA Modules:
  0.0 582.4 jit_solution(5943541975965832612)
XLA Ops:
  14.8 3.0 copy.74
  18.6 13.8 %all_gather.24 = bf16[2048,128]{1,0:T(8,128)(2,1)S(1)} all-gather(bf16[256,128]{1,0:T(8,128)(2,1)S(1)} %copy-done.6), channel_id=1, replica_groups=mesh['seq'=32,'head'=8] {'head'}, dimensions={0}, use_global_device_ids=true | all-gather | bytes 589824 | tf_op jit(solution)/shard_map/all_gather | solution.py:83
  32.7 3.3 fusion.90
  40.6 74.1 %all-reduce = f32[320]{0:T(512)S(1)} all-reduce(f32[320]{0:T(512)S(1)} %dynamic-update-slice), channel_id=2, replica_groups=mesh['seq'=32,'head'=8] {'seq'}, use_global_device_ids=true, to_apply=%add | all-reduce | flops 320 | bytes 2560
  114.8 5.1 copy.94
  119.9 3.9 copy.78
  123.9 4.4 copy.72
  133.2 4.9 copy.95
  144.9 3.1 collective-permute-start.5
  150.0 4.7 collective-permute-done.6
  155.8 3.3 fusion.87
  159.2 3.1 while.81
  162.6 118.5 %while.83 = (s32[]{:T(128)}, f32[10,128,64]{1,2,0:T(8,128)S(1)}, f32[8,128,256]{1,2,0:T(8,128)}, f32[8,10,256,256]{3,2,1,0:T(8,128)}, f32[8,10,1,256]{3,1,2,0:T(...) while((s32[]{:T(128)}, f32[10,128,64]{1,2,0:T(8,128)S(1)}, ...), condition=%wide.region_14.15_spmd.clone.clone, body=%wide.region_9.14_spmd.clone.sunk.clone | while | flops 356031040 | bytes 10220163 | solution.py:132
  165.6 3.1 multiply_dynamic-update-slice_fusion.3
  180.5 3.1 multiply_dynamic-update-slice_fusion.3
  210.1 3.0 multiply_dynamic-update-slice_fusion.3
  225.0 3.0 multiply_dynamic-update-slice_fusion.3
  239.8 3.0 multiply_dynamic-update-slice_fusion.3
  254.6 3.0 multiply_dynamic-update-slice_fusion.3
  281.2 42.3 %while.80 = (s32[]{:T(128)}, f32[10,128,64]{2,1,0:T(8,128)S(1)}, s32[]{:T(128)}, f32[32,10]{1,0:T(8,128)S(1)}, f32[32,10,128,64]{2,3,1,0:T(8,128)}) while((s32[]{:T(128)}, f32[10,128,64]{2,1,0:T(8,128)S(1)}, s32[]{:T(128)}, f32[32,10]{1,0:T(8,128)S(1)}, f32[32,10,128,64]{2,3,1,0:T(8,128)}) %tuple.184), condition=%wide.region_6.7_spmd.clone, body=%wide.region_5.6_spmd.sunk.clone | while | flops 163846 | bytes 2293995 | solution.py:43
  323.9 183.6 %while.82 = (s32[]{:T(128)}, f32[10,128,64]{1,2,0:T(8,128)S(1)}, bf16[8,256,10,64]{1,3,2,0:T(8,128)(2,1)}, f32[8,256,128]{2,1,0:T(8,128)S(1)}, f32[8,256,128]{2,...) while((s32[]{:T(128)}, f32[10,128,64]{1,2,0:T(8,128)S(1)}, ...), condition=%wide.region_17.18_spmd.clone, body=%wide.region_15.17_spmd.sunk.clone | while | flops 2217705472 | bytes 16956240 | solution.py:132
  323.9 3.0 constant_dynamic-slice_fusion.18
  328.4 4.2 fusion.184
  333.3 4.4 fusion.185
  346.8 3.0 constant_dynamic-slice_fusion.18
  351.3 4.2 fusion.184
  356.3 4.4 fusion.185
  369.8 3.0 constant_dynamic-slice_fusion.18
  374.3 4.2 fusion.184
  379.2 4.4 fusion.185
  392.7 3.0 constant_dynamic-slice_fusion.18
  397.2 4.2 fusion.184
  402.1 4.4 fusion.185
  415.7 3.0 constant_dynamic-slice_fusion.18
  420.2 4.2 fusion.184
  425.1 4.4 fusion.185
  438.6 3.0 constant_dynamic-slice_fusion.18
  443.1 4.2 fusion.184
  448.0 4.4 fusion.185
  461.6 3.0 constant_dynamic-slice_fusion.18
  466.1 4.2 fusion.184
  471.0 4.4 fusion.185
  484.5 3.0 constant_dynamic-slice_fusion.18
  489.0 4.2 fusion.184
  493.9 4.4 fusion.185
  509.0 3.4 copy.83
  515.9 23.7 %reduce-scatter.3.cloned.1.call-done = f32[256,128]{1,0:T(8,128)} async-done(((f32[2048,128]{1,0:T(8,128)}), f32[256,128]{1,0:T(8,128)}) %reduce-scatter.3.cloned.1.call-update) | async-done | bytes 131088 | tf_op jit(solution)/shard_map/reduce_scatter | solution.py:140
  539.6 36.3 %reduce-scatter.5.cloned.1.call-done = f32[256,128]{1,0:T(8,128)} async-done(((f32[2048,128]{1,0:T(8,128)}), f32[256,128]{1,0:T(8,128)}) %reduce-scatter.5.cloned.1.call-update) | async-done | bytes 131088 | tf_op jit(solution)/shard_map/reduce_scatter | solution.py:141
  (545 shorter events, 260.6 us)
Async XLA Ops:
  7.2 152.0 %all-gather.8.cloned.1.call-start = ((), (), s32[]{:S(2)}) async-start(), calls=%async_computation.5 | async-start | bytes 10813440 | tf_op jit(solution)/shard_map/all_gather | solution.py:34
  14.8 3.7 copy-start.6
  17.8 14.7 %copy-start.5 = (f32[10,2048]{1,0:T(8,128)S(1)}, f32[10,2048]{1,0:T(8,128)}, u32[]{:S(2)}) copy-start(f32[10,2048]{1,0:T(8,128)} %param.18) | copy-start | bytes 245764
  18.5 14.1 %copy-start = (f32[2048,640]{0,1:T(8,128)}, f32[2048,640]{0,1:T(8,128)S(1)}, u32[]{:S(2)}) copy-start(f32[2048,640]{0,1:T(8,128)S(1)} %convert_element_type.76) | copy-start | bytes 15728644
  18.5 17.5 %copy-start.7 = (bf16[256,128]{1,0:T(8,128)(2,1)S(1)}, bf16[256,128]{1,0:T(8,128)(2,1)}, u32[]{:S(2)}) copy-start(bf16[256,128]{1,0:T(8,128)(2,1)} %param.17) | copy-start | bytes 196612
  18.5 20.5 %copy-start.9 = (u32[256]{0:T(256)S(1)}, u32[256]{0:T(256)}, u32[]{:S(2)}) copy-start(u32[256]{0:T(256)} %constant.261) | copy-start | bytes 3076
  36.0 245.1 %all-gather.6.cloned.1.call-start = ((), (), s32[]{:S(2)}) async-start(), calls=%async_computation.4 | async-start | bytes 10813440 | tf_op jit(solution)/shard_map/all_gather | solution.py:34
  36.1 103.9 %collective-permute-start = (bf16[256,128]{1,0:T(8,128)(2,1)S(1)}, bf16[256,128]{1,0:T(8,128)(2,1)S(1)}, u32[]{:S(2)}, u32[]{:S(2)}) collective-permute-start(bf16[256,128]{1,0:T(8,128)(2,1)S(1)} %copy-done.7), channel_id=1, source_target_pairs={{0,1},{1,2},{2,3},{3,4},{4,5},{5,6},{6,7},{7,0},{8,9},{9,10},{10,1... | collective-permute-start | bytes 196616 | tf_op jit(solution)/shard_map/ppermute | solution.py:18
  36.4 103.6 %collective-permute-start.1 = (bf16[256,128]{1,0:T(8,128)(2,1)S(1)}, bf16[256,128]{1,0:T(8,128)(2,1)S(1)}, u32[]{:S(2)}, u32[]{:S(2)}) collective-permute-start(bf16[256,128]{1,0:T(8,128)(2,1)S(1)} %copy-done.7), channel_id=1, source_target_pairs={{0,7},{1,0},{2,1},{3,2},{4,3},{5,4},{6,5},{7,6},{8,15},{9,8},{10,9... | collective-permute-start | bytes 196616 | tf_op jit(solution)/shard_map/ppermute | solution.py:23
  130.8 2.4 copy-start.1
  138.0 17.7 %copy-start.2 = (f32[2048,640]{0,1:T(8,128)S(1)}, f32[2048,640]{0,1:T(8,128)}, u32[]{:S(2)}) copy-start(f32[2048,640]{0,1:T(8,128)} %copy-done.1) | copy-start | bytes 15728644
  140.0 4.9 collective-permute-start.2
  140.0 4.9 collective-permute-start.3
  144.9 4.9 collective-permute-start.4
  144.9 5.1 collective-permute-start.5
  149.8 4.9 collective-permute-start.6
  159.1 380.4 %reduce-scatter.3.cloned.1.call-start = ((), (), s32[]{:S(2)}) async-start(), calls=%async_computation.2 | async-start | bytes 1179648 | tf_op jit(solution)/shard_map/reduce_scatter | solution.py:140
  281.2 42.7 %copy-start.8 = (f32[10]{0:T(128)S(1)}, f32[10]{0:T(128)}, u32[]{:S(2)}) copy-start(f32[10]{0:T(128)} %param.19) | copy-start | bytes 124
  507.4 1.0 copy-start.3
  507.5 1.3 copy-start.4
  508.5 67.4 %reduce-scatter.5.cloned.1.call-start = ((), (), s32[]{:S(2)}) async-start(), calls=%async_computation.3 | async-start | bytes 1179648 | tf_op jit(solution)/shard_map/reduce_scatter | solution.py:141
Sparse Core Ops, SparseCore 0:
  36.1 110.0 all-gather.7
  159.2 103.9 all-gather.5
  508.6 30.9 reduce-scatter.2
  542.5 33.3 reduce-scatter.4
